TPU v7x, 32 devices: a whole 2x2x4 slice. The times are simulated.
32 devices in a mesh: seq: 4 (over x, core), hid: 8 (over z, y).
Axes of the slice: x: 2, y: 2, z: 4, core: 2. Of those that a mesh axis runs over, the one named last changes fastest.
Arguments:
- stream: bfloat16 [2048, 2048], P('seq'), may hold values from -5 to 5
- queries: bfloat16 [2048, 16, 128], P('seq', 'hid'), may hold values from -150 to 150
- key_rows: bfloat16 [2048, 16, 128], P('seq', 'hid'), may hold values from -5 to 5
- value_rows: bfloat16 [2048, 16, 128], P('seq', 'hid'), may hold values from -5 to 5
- segment_ids: int32 [2048], replicated, may hold values from 0 to 3, never falling along the last dimension, each value on 1 to 1024 neighbouring positions
- out_proj: bfloat16 [16, 128, 2048], P('hid'), may hold values from -0.125 to 0.125
- norm_gain: float32 [2048], replicated, may hold values from 0.1 to 1.9
- expert_ids: int32 [2048, 6], P('seq'), may hold values from 0 to 63, all different within a row; in each aligned block of 512 rows (0 to 511, 512 to 1023, ...) at most 64 rows name the same one
- route_gates: float32 [2048, 6], P('seq'), may hold values from 0.05 to 0.4
- gate_proj: bfloat16 [90112, 2048], P(('seq', 'hid')), may hold values from -0.125 to 0.125
- up_proj: bfloat16 [90112, 2048], P(('seq', 'hid')), may hold values from -0.125 to 0.125
- down_proj: bfloat16 [90112, 2048], P(('seq', 'hid')), may hold values from -0.15625 to 0.15625
- shared_gate: bfloat16 [2816, 2048], P('hid'), may hold values from -0.125 to 0.125
- shared_up: bfloat16 [2816, 2048], P('hid'), may hold values from -0.125 to 0.125
- shared_down: bfloat16 [2816, 2048], P('hid'), may hold values from -0.109375 to 0.109375
Outputs:
- layer_out: bfloat16 [2048, 2048], P('seq', 'hid')
Inputs may be any that keep to these rules, and one draw needn't show every extreme that they name: `segment_ids`: segment numbers never fall along the tokens; every segment has at most 1024 tokens and one has exactly 1024. `expert_ids`: the 6 experts of a token differ; among the 512 tokens of one index of seq no expert is named by more than 64 tokens, a bound that some block reaches of them.
All inputs are finite; a program needn't handle non-finite values.
Results may differ from a plain program's by a relative error of at most 0.019.
Values may be sent and summed in bfloat16 or wider, within the bound.
A program may use at most 128 MiB of HBM per device.

v0:
```python
import jax
import jax.numpy as jnp
from jax import lax
from jax.sharding import PartitionSpec as P

EXPERTS = 64
FF = 1408
TOP = 6
CAP = 64


def on_device(
    stream,
    queries,
    key_rows,
    value_rows,
    segment_ids,
    out_proj,
    norm_gain,
    expert_ids,
    route_gates,
    gate_proj,
    up_proj,
    down_proj,
    shared_gate,
    shared_up,
    shared_down,
):
    tok_count = queries.shape[0]
    local_heads = queries.shape[1]
    head_width = queries.shape[2]
    width = stream.shape[1]
    inv_root = head_width ** (-0.5)
    seq_count = lax.axis_size("seq")
    hid_count = lax.axis_size("hid")
    hid_index = lax.axis_index("hid")
    query_first = lax.axis_index("seq") * tok_count
    query_seg = lax.dynamic_slice_in_dim(segment_ids, query_first, tok_count)
    query_pos = query_first + jnp.arange(tok_count, dtype=jnp.int32)
    run_max = jnp.full((tok_count, local_heads), -1e30, jnp.float32)
    key_part = lax.all_gather(key_rows, "seq", axis=0, tiled=True)
    value_part = lax.all_gather(value_rows, "seq", axis=0, tiled=True)
    row_count = key_part.shape[0]
    key_pos = jnp.arange(row_count, dtype=jnp.int32)
    scores = (
        jnp.einsum("qhd,khd->qhk", queries, key_part, preferred_element_type=jnp.float32) * inv_root
    )
    allowed = (query_seg[:, None] == segment_ids[None, :]) & (
        key_pos[None, :] <= query_pos[:, None]
    )
    scores = jnp.where(allowed[:, None, :], scores, -1e30)
    new_max = jnp.maximum(run_max, jnp.max(scores, axis=2))
    weights = jnp.where(allowed[:, None, :], jnp.exp(scores - new_max[:, :, None]), 0.0)
    new_sum = jnp.sum(weights, axis=2)
    probs = weights.astype(jnp.bfloat16)
    new_acc = jnp.einsum("qhk,khd->qhd", probs, value_part, preferred_element_type=jnp.float32)
    attended = (
        (new_acc / new_sum[:, :, None])
        .astype(jnp.bfloat16)
        .reshape(tok_count, local_heads * head_width)
    )
    out_flat = out_proj.reshape(local_heads * head_width, width)
    partial_mix = jnp.dot(attended, out_flat, preferred_element_type=jnp.float32)
    mixed = stream.astype(jnp.float32) + lax.psum(partial_mix.astype(jnp.bfloat16), "hid").astype(
        jnp.float32
    )
    mean_square = jnp.mean(mixed * mixed, axis=1, keepdims=True)
    normed = (mixed * lax.rsqrt(mean_square + 1e-06) * norm_gain).astype(jnp.bfloat16)
    shared_gate_val = jnp.einsum(
        "td,fd->tf", normed, shared_gate, preferred_element_type=jnp.float32
    )
    shared_up_val = jnp.einsum("td,fd->tf", normed, shared_up, preferred_element_type=jnp.float32)
    shared_act = (jax.nn.silu(shared_gate_val) * shared_up_val).astype(jnp.bfloat16)
    shared_part = jnp.dot(shared_act, shared_down, preferred_element_type=jnp.float32)
    shared_out = lax.psum_scatter(
        shared_part.astype(jnp.bfloat16), "hid", scatter_dimension=1, tiled=True
    ).astype(jnp.float32)
    col_count = shared_out.shape[1]
    unit_rows = gate_proj.shape[0]
    held_count = max(1, unit_rows // FF)
    held_units = unit_rows // held_count
    local_experts = EXPERTS // seq_count
    first_local = hid_index * unit_rows // FF
    flat_ids = expert_ids.reshape(-1)
    onehot = (flat_ids[:, None] == jnp.arange(EXPERTS, dtype=jnp.int32)[None, :]).astype(jnp.int32)
    slot_rank = jnp.sum((jnp.cumsum(onehot, axis=0) - 1) * onehot, axis=1)
    owner_group = flat_ids // local_experts
    local_expert = flat_ids % local_experts
    held_offset = local_expert - first_local
    is_held = (held_offset >= 0) & (held_offset < held_count)
    slot_total = seq_count * held_count * CAP
    send_index = jnp.where(
        is_held, (owner_group * held_count + held_offset) * CAP + slot_rank, slot_total
    )
    route_token = jnp.arange(tok_count * TOP, dtype=jnp.int32) // TOP
    slot_token = jnp.full((slot_total,), -1, jnp.int32).at[send_index].set(route_token, mode="drop")
    send_rows = jnp.where(
        (slot_token >= 0)[:, None], normed[jnp.maximum(slot_token, 0)], jnp.zeros((), jnp.bfloat16)
    )
    send_rows = send_rows.reshape(seq_count, held_count, CAP, width)
    received = lax.all_to_all(send_rows, "seq", split_axis=0, concat_axis=0, tiled=True)
    gate_local = gate_proj.reshape(held_count, held_units, width)
    up_local = up_proj.reshape(held_count, held_units, width)
    down_local = down_proj.reshape(held_count, held_units, hid_count, col_count)
    gate_val = jnp.einsum(
        "sicd,ifd->sicf", received, gate_local, preferred_element_type=jnp.float32
    )
    up_val = jnp.einsum("sicd,ifd->sicf", received, up_local, preferred_element_type=jnp.float32)
    expert_act = (jax.nn.silu(gate_val) * up_val).astype(jnp.bfloat16)
    down_part = jnp.einsum(
        "sicf,ifnx->niscx", expert_act, down_local, preferred_element_type=jnp.float32
    ).astype(jnp.bfloat16)
    down_part = down_part.reshape(hid_count, held_count, seq_count * CAP, col_count)
    peer_parts = lax.all_to_all(down_part, "hid", split_axis=0, concat_axis=0, tiled=True)
    part_count = hid_count * held_count // local_experts
    expert_out = jnp.sum(
        peer_parts.reshape(local_experts, part_count, seq_count * CAP, col_count).astype(
            jnp.float32
        ),
        axis=1,
    ).astype(jnp.bfloat16)
    returned = lax.all_to_all(
        expert_out.reshape(local_experts, seq_count, CAP, col_count),
        "seq",
        split_axis=1,
        concat_axis=1,
        tiled=True,
    ).reshape(-1, col_count)
    pick_index = local_expert * (seq_count * CAP) + owner_group * CAP + slot_rank
    picked = returned[pick_index].reshape(tok_count, TOP, col_count)
    routed_sum = jnp.einsum("tj,tjd->td", route_gates, picked.astype(jnp.float32))
    mixed_cols = lax.dynamic_slice_in_dim(mixed, hid_index * col_count, col_count, 1)
    return (mixed_cols + shared_out + routed_sum).astype(jnp.bfloat16)


def solution(mesh):
    placed = (
        P("seq", None),
        P("seq", "hid", None),
        P("seq", "hid", None),
        P("seq", "hid", None),
        P(),
        P("hid", None, None),
        P(),
        P("seq", None),
        P("seq", None),
        P(("seq", "hid"), None),
        P(("seq", "hid"), None),
        P(("seq", "hid"), None),
        P("hid", None),
        P("hid", None),
        P("hid", None),
    )
    return jax.shard_map(
        on_device, mesh=mesh, in_specs=placed, out_specs=P("seq", "hid"), check_vma=False
    )
```

profile of v0, /device:TPU:9, one launch (start us, length us, event | category | flops | bytes accessed | tf_op | source)
XLA Modules:
  0.0 353.1 jit_solution(15966654541376554289)
XLA Ops:
  10.8 18.3 %reduce-window.6 = s32[64,24,128]{2,1,0:T(8,128)S(1)} reduce-window(s32[64,24,128]{2,1,0:T(8,128)S(1)} %fusion.37, s32[]{:T(128)} %constant.43.clone.1), window={size=1x1x128 pad=0_0x0_0x127_0}, to_apply=%region_5.6 | reduce-window | flops 24969216 | bytes 1572868 | tf_op jit(solution)/shard_map/reduce-window
  35.4 3.2 copy-done.4
  40.8 4.9 %all-gather.5.cloned.1.call-done = bf16[2048,2,128]{2,1,0:T(2,128)(2,1)} async-done(((bf16[512,2,128]{2,1,0:T(2,128)(2,1)}), bf16[2048,2,128]{2,1,0:T(2,128)(2,1)}) %all-gather.5.cloned.1.call-update) | async-done | bytes 1048592 | tf_op jit(solution)/shard_map/all_gather | solution.py:42
  45.7 8.9 %bitcast_convert_fusion = bf16[512,2048]{1,0:T(8,128)(2,1)} fusion(bf16[2,128,2048]{2,1,0:T(8,128)(2,1)} %param.20, bf16[2048,2,128]{2,1,0:T(2,128)(2,1)} %all-gather.5.cloned.1.call-done, f32[2,2048,512]{2,1,0:T(8,128)} %copy-done.4, f32[512,2]{0,1:T(2,128)S(1)} %broadcast_maximum_fusion, pred[512,2048]{0,1:T(8,128)(4,1)S(1)} %fusion.7, ...), kind=kOutput, calls=%fused_computation.11 | convolution fusion | flops 1085538304 | bytes 13639680 | tf_op jit(solution)/shard_map/dot_general | solution.py:63
  60.2 12.1 %scatter_custom_fusion = s32[512]{0:T(512)S(1)} fusion(s32[3072]{0:T(1024)S(1)} %bitcast.115, s32[3072]{0:T(1024)} %add_select_fusion, s32[]{:T(128)} %constant.87.clone.1), kind=kCustom, calls=%fused_computation.75 | custom fusion | bytes 2560 | tf_op jit(solution)/shard_map/scatter | solution.py:96
  72.4 83.5 %all-reduce.2.cloned.1.call-done = bf16[512,2048]{1,0:T(8,128)(2,1)} async-done(((bf16[512,2048]{1,0:T(8,128)(2,1)}), bf16[512,2048]{1,0:T(8,128)(2,1)}) %all-reduce.2.cloned.1.call-update) | async-done | bytes 2097168 | tf_op jit(solution)/shard_map/psum | solution.py:64
  156.0 4.4 %convert_add_fusion = (f32[512,2048]{1,0:T(8,128)}, f32[512]{0:T(512)S(1)}) fusion(bf16[512,2048]{1,0:T(8,128)(2,1)} %all-reduce.2.cloned.1.call-done, bf16[512,2048]{1,0:T(8,128)(2,1)S(1)} %copy-done.1), kind=kLoop, calls=%fused_computation.14 | loop fusion | flops 5242368 | bytes 8390656 | tf_op jit(solution)/shard_map/add | solution.py:64
  161.6 3.3 gather_fusion
  164.9 3.1 broadcast_select_fusion
  168.0 5.3 %all-to-all-start = ((bf16[4,2,64,2048]{3,2,1,0:T(8,128)(2,1)}), bf16[4,2,64,2048]{3,2,1,0:T(8,128)(2,1)}, u32[]{:S(2)}, u32[]{:S(2)}) async-start(bf16[4,2,64,2048]{3,2,1,0:T(8,128)(2,1)} %broadcast_select_fusion), calls=%async_computation.1 | async-start | bytes 4194304 | tf_op jit(solution)/shard_map/all_to_all | solution.py:101
  173.3 7.7 %copy.56 = bf16[352,8,8,256]{3,2,1,0:T(8,128)(2,1)S(1)} copy(bf16[352,8,8,256]{3,1,2,0:T(8,128)(2,1)} %bitcast.105) | data formatting | bytes 23068672
  181.1 4.9 %bitcast_bitcast_fusion = bf16[2,1408,8,256,1]{3,2,1,0,4:T(8,128)(2,1)} fusion(bf16[2,1408,8,256]{3,2,1,0:T(8,128)(2,1)S(1)} %bitcast.104), kind=kLoop, calls=%fused_computation.3 | loop fusion | bytes 23068672 | tf_op jit(solution)/shard_map/reshape | solution.py:104
  186.0 12.3 %all-to-all-done = bf16[4,2,64,2048]{3,2,1,0:T(8,128)(2,1)} async-done(((bf16[4,2,64,2048]{3,2,1,0:T(8,128)(2,1)}), bf16[4,2,64,2048]{3,2,1,0:T(8,128)(2,1)}, u32[]{:S(2)}, u32[]{:S(2)}) %all-to-all-start) | async-done | bytes 2097184 | tf_op jit(solution)/shard_map/all_to_all | solution.py:101
  198.3 7.4 %convolution_bitcast_fusion.1 = f32[4,2,64,1408]{3,2,0,1:T(8,128)S(1)} fusion(bf16[2,1408,2048,1]{2,1,3,0:T(8,128)(2,1)} %bitcast.116, bf16[4,2,64,2048]{3,2,1,0:T(8,128)(2,1)} %all-to-all-done), kind=kOutput, calls=%fused_computation.21 | convolution fusion | flops 2952790016 | bytes 16515072 | tf_op jit(solution)/shard_map/sicd,ifd->sicf/dot_general | solution.py:105
  205.6 8.8 %fusion.11 = bf16[4,2,64,1408,1]{3,2,4,0,1:T(8,128)(2,1)S(1)} fusion(bf16[2,1408,2048,1]{2,1,3,0:T(8,128)(2,1)} %bitcast.117, f32[4,2,64,1408]{3,2,0,1:T(8,128)S(1)} %convolution_bitcast_fusion.1, bf16[4,2,64,2048]{3,2,1,0:T(8,128)(2,1)} %all-to-all-done), kind=kOutput, calls=%fused_computation.24 | convolution fusion | flops 2957115392 | bytes 17956864 | tf_op jit(solution)/shard_map/sicd,ifd->sicf/dot_general | solution.py:108
  214.4 7.7 %convert_bitcast_fusion = bf16[8,2,4,64,256]{4,3,0,2,1:T(8,128)(2,1)S(1)} fusion(bf16[4,2,64,1408,1]{3,2,4,0,1:T(8,128)(2,1)S(1)} %fusion.11, bf16[2,1408,8,256,1]{3,2,1,0,4:T(8,128)(2,1)} %bitcast_bitcast_fusion), kind=kOutput, calls=%fused_computation.25 | convolution fusion | flops 2953838592 | bytes 15073280 | tf_op jit(solution)/shard_map/sicf,ifnx->niscx/dot_general | solution.py:110
  223.7 4.5 %all-to-all-start.1 = ((bf16[8,2,256,256]{3,2,1,0:T(8,128)(2,1)}), bf16[8,2,256,256]{3,2,1,0:T(8,128)(2,1)}, u32[]{:S(2)}, u32[]{:S(2)}) async-start(bf16[8,2,256,256]{3,2,1,0:T(8,128)(2,1)} %bitcast.107), calls=%async_computation.2 | async-start | bytes 4194304 | tf_op jit(solution)/shard_map/all_to_all | solution.py:114
  228.3 3.2 fusion.60
  231.4 5.1 %convolution_convert_fusion = bf16[512,2048]{1,0:T(8,128)(2,1)} fusion(bf16[352,2048]{1,0:T(8,128)(2,1)S(1)} %copy-done, bf16[512,2048]{1,0:T(8,128)(2,1)S(1)} %multiply_convert_fusion, bf16[352,2048]{1,0:T(8,128)(2,1)} %param.28, f32[512,352]{0,1:T(8,128)} %fusion.60), kind=kOutput, calls=%fused_computation.23 | convolution fusion | flops 1478524928 | bytes 7798784 | tf_op jit(solution)/shard_map/dot_general | solution.py:74
  236.5 55.1 %all-to-all-done.1 = bf16[8,2,256,256]{3,2,1,0:T(8,128)(2,1)} async-done(((bf16[8,2,256,256]{3,2,1,0:T(8,128)(2,1)}), bf16[8,2,256,256]{3,2,1,0:T(8,128)(2,1)}, u32[]{:S(2)}, u32[]{:S(2)}) %all-to-all-start.1) | async-done | bytes 2097184 | tf_op jit(solution)/shard_map/all_to_all | solution.py:114
  291.7 3.2 copy.43
  294.8 5.0 %all-to-all-start.2 = ((bf16[16,4,64,256]{3,2,0,1:T(8,128)(2,1)}), bf16[16,4,64,256]{3,2,0,1:T(8,128)(2,1)}, u32[]{:S(2)}, u32[]{:S(2)}) async-start(bf16[16,4,64,256]{3,2,0,1:T(8,128)(2,1)} %copy.43), calls=%async_computation.3 | async-start | bytes 4194304 | tf_op jit(solution)/shard_map/all_to_all | solution.py:122
  300.8 24.0 %all-to-all-done.2 = bf16[16,4,64,256]{3,2,0,1:T(8,128)(2,1)} async-done(((bf16[16,4,64,256]{3,2,0,1:T(8,128)(2,1)}), bf16[16,4,64,256]{3,2,0,1:T(8,128)(2,1)}, u32[]{:S(2)}, u32[]{:S(2)}) %all-to-all-start.2) | async-done | bytes 2097184 | tf_op jit(solution)/shard_map/all_to_all | solution.py:122
  326.5 13.0 %gather_fusion.1 = bf16[3072,256]{1,0:T(8,128)(2,1)} fusion(bf16[4096,256]{1,0:T(8,128)(2,1)S(1)} %bitcast.103, s32[3072]{0:T(1024)S(1)} %broadcast_clamp_fusion), kind=kCustom, calls=%fused_computation.1 | custom fusion | bytes 3158016 | tf_op jit(solution)/shard_map/gather | solution.py:130
  (62 shorter events, 30.8 us)
Async XLA Ops:
  6.5 224.9 %copy-start = (bf16[352,2048]{1,0:T(8,128)(2,1)S(1)}, bf16[352,2048]{1,0:T(8,128)(2,1)}, u32[]{:S(2)}) copy-start(bf16[352,2048]{1,0:T(8,128)(2,1)} %param.29) | copy-start | bytes 4325380
  6.5 25.7 %all-gather.3.cloned.1.call-start = ((), (), s32[]{:S(2)}) async-start(), calls=%async_computation.4 | async-start | bytes 1310720 | tf_op jit(solution)/shard_map/all_gather | solution.py:41
  8.4 21.7 %copy-start.8 = (s32[2048]{0:T(1024)S(1)}, s32[2048]{0:T(1024)}, u32[]{:S(2)}) copy-start(s32[2048]{0:T(1024)} %param.19) | copy-start | bytes 24580
  8.4 37.3 %all-gather.5.cloned.1.call-start = ((), (), s32[]{:S(2)}) async-start(), calls=%async_computation.5 | async-start | bytes 1310720 | tf_op jit(solution)/shard_map/all_gather | solution.py:42
  9.1 146.8 %all-reduce.2.cloned.1.call-start = ((), (), s32[]{:S(2)}) async-start(), calls=%async_computation.6 | async-start | bytes 4194304 | tf_op jit(solution)/shard_map/psum | solution.py:64
  10.1 0.7 copy-start.5
  35.3 3.2 copy-start.4
  54.6 101.4 %copy-start.1 = (bf16[512,2048]{1,0:T(8,128)(2,1)S(1)}, bf16[512,2048]{1,0:T(8,128)(2,1)}, u32[]{:S(2)}) copy-start(bf16[512,2048]{1,0:T(8,128)(2,1)} %param.15) | copy-start | bytes 6291460
  72.4 88.0 %copy-start.9 = (f32[2048]{0:T(1024)S(1)}, f32[2048]{0:T(1024)}, u32[]{:S(2)}) copy-start(f32[2048]{0:T(1024)} %param.21) | copy-start | bytes 24580
  156.0 4.5 %copy-start.2 = (bf16[512,2048]{1,0:T(8,128)(2,1)S(1)}, bf16[512,2048]{1,0:T(8,128)(2,1)}, u32[]{:S(2)}) copy-start(bf16[512,2048]{1,0:T(8,128)(2,1)} %param.15) | copy-start | bytes 6291460
  156.0 4.5 %copy-start.3 = (bf16[512,2048]{1,0:T(8,128)(2,1)S(1)}, bf16[512,2048]{1,0:T(8,128)(2,1)}, u32[]{:S(2)}) copy-start(bf16[512,2048]{1,0:T(8,128)(2,1)} %all-reduce.2.cloned.1.call-done) | copy-start | bytes 6291460
  168.0 30.2 %all-to-all-start = ((bf16[4,2,64,2048]{3,2,1,0:T(8,128)(2,1)}), bf16[4,2,64,2048]{3,2,1,0:T(8,128)(2,1)}, u32[]{:S(2)}, u32[]{:S(2)}) async-start(bf16[4,2,64,2048]{3,2,1,0:T(8,128)(2,1)} %broadcast_select_fusion), calls=%async_computation.1 | async-start | bytes 4194304 | tf_op jit(solution)/shard_map/all_to_all | solution.py:101
  223.7 68.0 %all-to-all-start.1 = ((bf16[8,2,256,256]{3,2,1,0:T(8,128)(2,1)}), bf16[8,2,256,256]{3,2,1,0:T(8,128)(2,1)}, u32[]{:S(2)}, u32[]{:S(2)}) async-start(bf16[8,2,256,256]{3,2,1,0:T(8,128)(2,1)} %bitcast.107), calls=%async_computation.2 | async-start | bytes 4194304 | tf_op jit(solution)/shard_map/all_to_all | solution.py:114
  228.2 116.2 %reduce-scatter.2.cloned.1.call-start = ((), (), s32[]{:S(2)}) async-start(), calls=%async_computation.7 | async-start | bytes 2359296 | tf_op jit(solution)/shard_map/reduce_scatter | solution.py:75
  294.8 5.0 %copy-start.7 = (f32[512,6]{0,1:T(8,128)S(1)}, f32[512,6]{0,1:T(8,128)}, u32[]{:S(2)}) copy-start(f32[512,6]{0,1:T(8,128)} %param.23) | copy-start | bytes 36868
  294.8 6.0 %copy-start.6 = (s32[3072,1]{0,1:T(1,128)S(1)}, s32[3072,1]{0,1:T(1,128)}, u32[]{:S(2)}) copy-start(s32[3072,1]{0,1:T(1,128)} %get-tuple-element.5) | copy-start | bytes 36868
  294.8 30.0 %all-to-all-start.2 = ((bf16[16,4,64,256]{3,2,0,1:T(8,128)(2,1)}), bf16[16,4,64,256]{3,2,0,1:T(8,128)(2,1)}, u32[]{:S(2)}, u32[]{:S(2)}) async-start(bf16[16,4,64,256]{3,2,0,1:T(8,128)(2,1)} %copy.43), calls=%async_computation.3 | async-start | bytes 4194304 | tf_op jit(solution)/shard_map/all_to_all | solution.py:122
Sparse Core Ops, SparseCore 0:
  8.9 18.3 all-gather.2
  28.9 16.7 all-gather.4
  54.7 101.1 all-reduce.1
  236.7 89.0 reduce-scatter.1
where the time goes:
time: 358 us; the launch traced here: 353 us
  waiting for transfers between devices  180 us (50%)
  local copies, waits for them, and re-layouts  61.4 us (17%)
  matrix products  46.5 us (13%)
  other arithmetic  36.4 us (10%)
  starting transfers between devices  15 us (4%)
  between operations  13.3 us (4%)
    psum x1, waiting for transfers between devices, on_device(): lax.psum(partial_mix.astype(jnp.bfloat16), 'hid').astype(jnp.float32)  83.5 us
    all_to_all x1, waiting for transfers between devices, on_device(): lax.all_to_all(down_part, 'hid', split_axis=0, concat_axis=0, tiled=True)  55.1 us
    all_to_all x1, waiting for transfers between devices, on_device(): lax.all_to_all(expert_out.reshape(local_experts, seq_count, CAP, col_coun...  24 us
    another operation x2, other arithmetic  18.5 us
    unnamed x24, local copies, waits for them, and re-layouts  15.1 us
    gather x1, local copies, waits for them, and re-layouts, on_device(): picked = returned[pick_index].reshape(tok_count, TOP, col_count)  13 us
    all_to_all x1, waiting for transfers between devices, on_device(): lax.all_to_all(send_rows, 'seq', split_axis=0, concat_axis=0, tiled=True)  12.3 us
    scatter x1, local copies, waits for them, and re-layouts, on_device(): jnp.full((slot_total,), -1, jnp.int32).at[send_index]  12.1 us
  transfers between devices with their start and end apart: 7, of which 5 were waited for; matrix products, arithmetic and copies ran while one was open for 26% of the time, Pallas kernels for 0%

commit v1 on v0

v1 whole, which is shorter than its diff:
```python
import functools

import jax
import jax.numpy as jnp
from jax import lax
from jax.experimental import pallas as pl
from jax.experimental.pallas import tpu as pltpu
from jax.sharding import PartitionSpec as P

EXPERTS = 64
FF = 1408
TOP = 6
CAP = 64
HZ = 4
MESH = pl.DeviceIdType.MESH
F32 = jnp.float32
BF16 = jnp.bfloat16


def wrap(value, count):
    return lax.rem(value + count, count)


def remote(src, dst, send, recv, seq, hid):
    return pltpu.make_async_remote_copy(
        src_ref=src,
        dst_ref=dst,
        send_sem=send,
        recv_sem=recv,
        device_id=(seq, hid),
        device_id_type=MESH,
    )


def greet(seq, hid):
    pl.semaphore_signal(
        pltpu.get_barrier_semaphore(), inc=1, device_id=(seq, hid), device_id_type=MESH
    )


def mix_kernel(
    ns, hy, rows, slots, cols,
    att, wout, stream, gain, route, sg, su, sd,
    x_out, sh_out,
    ysend, yrecv, zsend, zrecv, normed, dsend, drecv, ssend, srecv, mixed,
    y_s, y_r, z_s, z_r, az_s, az_r, ay_s, ay_r, d_s, d_r, s_s, s_r,
):
    s = lax.axis_index("seq")
    h = lax.axis_index("hid")
    z, y = h // hy, lax.rem(h, hy)
    for dz in range(1, HZ):
        greet(s, wrap(z + dz, HZ) * hy + y)
    for dy in range(1, hy):
        greet(s, z * hy + wrap(y + dy, hy))
    for k in range(1, ns):
        greet(wrap(s + k, ns), h)
    pl.semaphore_wait(pltpu.get_barrier_semaphore(), HZ - 1 + hy - 1 + ns - 1)

    def at(c):
        return pl.ds(pl.multiple_of(c * rows, rows), rows)

    def part(c):
        return jnp.dot(att[at(c), :], wout[...], preferred_element_type=F32)

    sent = []
    for i in range(HZ):
        zt = wrap(z + i + 1, HZ)
        for j in range(hy - 1):
            yt = wrap(y + j + 1, hy)
            ysend[i, j] = part(zt * hy + yt).astype(BF16)
            copy = remote(ysend.at[i, j], yrecv.at[i, j], y_s.at[i, j], y_r.at[i, j], s, z * hy + yt)
            copy.start()
            sent.append(copy)
    to_y, to_z, acc = list(sent), [], None
    for i in range(HZ):
        zt = wrap(z + i + 1, HZ)
        acc = part(zt * hy + y)
        for j in range(hy - 1):
            to_y[i * (hy - 1) + j].wait_recv()
            acc = acc + yrecv[i, j].astype(F32)
        if i < HZ - 1:
            zsend[i] = acc.astype(BF16)
            copy = remote(zsend.at[i], zrecv.at[i], z_s.at[i], z_r.at[i], s, zt * hy + y)
            copy.start()
            to_z.append(copy)
    sent += to_z
    acc = acc + stream[...].astype(F32)
    for copy, i in zip(to_z, range(HZ)):
        copy.wait_recv()
        acc = acc + zrecv[i].astype(F32)
    mixed[...] = acc
    mean_square = jnp.mean(acc * acc, axis=1, keepdims=True)
    normed[at(h), :] = (acc * lax.rsqrt(mean_square + 1e-06) * gain[...]).astype(BF16)

    def spread(c, i):
        made = []
        for j in range(hy - 1):
            yt = wrap(y + j + 1, hy)
            copy = remote(normed.at[at(c)], normed.at[at(c)], ay_s.at[i, j], ay_r.at[i, j], s, z * hy + yt)
            copy.start()
            made.append(copy)
        return made

    gathers = []
    for i in range(HZ - 1):
        zt = wrap(z + i + 1, HZ)
        copy = remote(normed.at[at(h)], normed.at[at(h)], az_s.at[i], az_r.at[i], s, zt * hy + y)
        copy.start()
        gathers.append(copy)
    sides = spread(h, HZ - 1)
    for i in range(HZ - 1):
        c = wrap(z - i - 1, HZ) * hy + y
        remote(normed.at[at(c)], normed.at[at(c)], az_s.at[i], az_r.at[i], s, h).wait_recv()
        sides += spread(c, i)
    for i in range(HZ):
        for j in range(hy - 1):
            src = wrap(z - i - 1, HZ) * hy + wrap(y - j - 1, hy)
            remote(normed.at[at(src)], normed.at[at(src)], ay_s.at[i, j], ay_r.at[i, j], s, h).wait_recv()
    sent += gathers + sides

    def picked(block):
        rows_of = route[pl.ds(pl.multiple_of(block * slots, slots), slots), :]
        return jnp.dot(rows_of, normed[...], preferred_element_type=F32).astype(BF16)

    to_seq = []
    for k in range(ns - 1):
        kt = wrap(s + ns - 1 - k, ns)
        dsend[k] = picked(kt)
        copy = remote(dsend.at[k], drecv.at[k], d_s.at[k], d_r.at[k], kt, h)
        copy.start()
        to_seq.append(copy)
    sent += to_seq

    nt = (((1,), (1,)), ((), ()))
    gate_val = lax.dot_general(normed[...], sg[...], nt, preferred_element_type=F32)
    up_val = lax.dot_general(normed[...], su[...], nt, preferred_element_type=F32)
    act = (gate_val / (1.0 + jnp.exp(-gate_val)) * up_val).astype(BF16)

    def shared(hid, hold, at_hold):
        at_cols = pl.ds(pl.multiple_of(hid * cols, cols), cols)
        hold[at_hold] = jnp.dot(act, sd[:, at_cols], preferred_element_type=F32)
        hold[at_hold, at(h), :] = hold[at_hold, at(h), :] + mixed[:, at_cols]

    to_side = []
    for zt in range(HZ):
        for j in range(hy - 1):
            yt = wrap(y + j + 1, hy)
            shared(zt * hy + yt, sh_out, zt)
            ssend[zt, j] = sh_out[zt].astype(BF16)
            copy = remote(ssend.at[zt, j], srecv.at[zt, j], s_s.at[zt, j], s_r.at[zt, j], s, z * hy + yt)
            copy.start()
            to_side.append(copy)
    sent += to_side
    for zt in range(HZ):
        shared(zt * hy + y, sh_out, zt)
        for j in range(hy - 1):
            to_side[zt * (hy - 1) + j].wait_recv()
            sh_out[zt] = sh_out[zt] + srecv[zt, j].astype(F32)
    x_out[s] = picked(s)
    for k in range(ns - 1):
        to_seq[k].wait_recv()
        x_out[wrap(s + k + 1, ns)] = drecv[k]
    for copy in sent:
        copy.wait_send()


def combine_kernel(
    ns, hy, slots, cols,
    eo, gates, sh,
    out,
    recv, zsend, zrecv, l_s, l_r, z_s, z_r,
):
    s = lax.axis_index("seq")
    h = lax.axis_index("hid")
    z, y = h // hy, lax.rem(h, hy)
    layer = ns * hy
    me = s * hy + y

    def hello(k, carry):
        peer = lax.rem(me + k, layer)
        greet(peer // hy, z * hy + lax.rem(peer, hy))
        return carry

    lax.fori_loop(1, layer, hello, 0)
    for dz in range(1, HZ):
        greet(s, wrap(z + dz, HZ) * hy + y)
    pl.semaphore_wait(pltpu.get_barrier_semaphore(), layer - 1 + HZ - 1)

    def chunk(block, hid):
        return eo.at[block, :, pl.ds(pl.multiple_of(hid * cols, cols), cols)]

    def outgoing(i, k):
        zt = wrap(z + i + 1, HZ)
        peer = lax.rem(me + k, layer)
        block, yt = peer // hy, lax.rem(peer, hy)
        return remote(chunk(block, zt * hy + yt), recv.at[i, me], l_s.at[i, k], l_r.at[i, k], block, z * hy + yt)

    def incoming(i, k):
        peer = lax.rem(me + layer - k, layer)
        return remote(recv.at[i, peer], recv.at[i, peer], l_s.at[i, k], l_r.at[i, k], s, h)

    for i in range(HZ):
        def start(k, carry, i=i):
            outgoing(i, layer - k).start()
            return carry

        lax.fori_loop(1, layer, start, 0)
        recv[i, me] = eo[s, :, pl.ds(pl.multiple_of((wrap(z + i + 1, HZ) * hy + y) * cols, cols), cols)]

    to_z, total = [], None
    for i in range(HZ):
        def land(k, carry, i=i):
            incoming(i, layer - k).wait_recv()
            return carry

        lax.fori_loop(1, layer, land, 0)
        zt = wrap(z + i + 1, HZ)
        total = sh[zt] + jnp.dot(
            gates[...], recv[i].reshape(layer * slots, cols), preferred_element_type=F32
        )
        if i < HZ - 1:
            zsend[i] = total.astype(BF16)
            copy = remote(zsend.at[i], zrecv.at[i], z_s.at[i], z_r.at[i], s, zt * hy + y)
            copy.start()
            to_z.append(copy)
    for i in range(HZ - 1):
        to_z[i].wait_recv()
        total = total + zrecv[i].astype(F32)
    out[...] = total.astype(BF16)
    for i in range(HZ):
        def left(k, carry, i=i):
            outgoing(i, k).wait_send()
            return carry

        lax.fori_loop(1, layer, left, 0)
    for copy in to_z:
        copy.wait_send()


def on_device(
    stream,
    queries,
    key_rows,
    value_rows,
    segment_ids,
    out_proj,
    norm_gain,
    expert_ids,
    route_gates,
    gate_proj,
    up_proj,
    down_proj,
    shared_gate,
    shared_up,
    shared_down,
):
    tok_count, local_heads, head_width = queries.shape
    width = stream.shape[1]
    ns = lax.axis_size("seq")
    nh = lax.axis_size("hid")
    hy = nh // HZ
    rows = tok_count // nh
    cols = width // nh
    seq_index = lax.axis_index("seq")
    hid_index = lax.axis_index("hid")
    z_index = hid_index // hy
    unit_rows = gate_proj.shape[0]
    held = max(1, unit_rows // FF)
    units = unit_rows // held
    local_experts = EXPERTS // ns
    slots = held * CAP

    experts = jnp.arange(EXPERTS, dtype=jnp.int32)
    named = expert_ids[:, :, None] == experts[None, None, :]
    member = jnp.any(named, axis=1).astype(BF16)
    gate_of = jnp.sum(jnp.where(named, route_gates[:, :, None], 0.0), axis=1).astype(BF16)
    place = jnp.arange(tok_count, dtype=jnp.int32)
    earlier = (place[None, :] < place[:, None]).astype(BF16)
    rank = jnp.dot(earlier, member, preferred_element_type=F32)
    rank = jnp.where(member > 0, rank, 128.0).astype(BF16)
    slot = jnp.arange(CAP, dtype=jnp.int32).astype(F32)
    held_at = jnp.arange(held, dtype=jnp.int32)
    mine = (
        jnp.arange(ns, dtype=jnp.int32)[:, None] * local_experts
        + hid_index * unit_rows // FF
        + held_at[None, :]
    ).reshape(-1)
    pick_mine = (experts[:, None] == mine[None, :]).astype(BF16)
    rank_mine = lax.dot_general(
        pick_mine, rank, (((0,), (1,)), ((), ())), preferred_element_type=F32
    )
    route = (
        (rank_mine[:, None, :] == slot[None, :, None])
        .astype(BF16)
        .reshape(ns * slots, tok_count)
    )
    layer_hid = z_index * hy + jnp.arange(hy, dtype=jnp.int32)
    layer = (
        jnp.arange(ns, dtype=jnp.int32)[:, None, None] * local_experts
        + (layer_hid * unit_rows // FF)[None, :, None]
        + held_at[None, None, :]
    ).reshape(-1)
    pick_layer = (experts[:, None] == layer[None, :]).astype(BF16)
    rank_layer = jnp.dot(rank, pick_layer, preferred_element_type=F32)
    gate_layer = jnp.dot(gate_of, pick_layer, preferred_element_type=F32)
    gates = (
        jnp.where(rank_layer[:, :, None] == slot[None, None, :], gate_layer[:, :, None], 0.0)
        .astype(BF16)
        .reshape(tok_count, ns * hy * slots)
    )

    query_first = seq_index * tok_count
    query_seg = lax.dynamic_slice_in_dim(segment_ids, query_first, tok_count)
    query_pos = query_first + place
    both = jnp.concatenate([key_rows, value_rows], axis=1).reshape(tok_count, -1)
    both = lax.all_gather(both, "seq", axis=0, tiled=True)
    both = both.reshape(-1, 2 * local_heads, head_width)
    keys, values = both[:, :local_heads], both[:, local_heads:]
    key_pos = jnp.arange(keys.shape[0], dtype=jnp.int32)
    allowed = (query_seg[:, None] == segment_ids[None, :]) & (
        key_pos[None, :] <= query_pos[:, None]
    )
    scores = jnp.einsum("qhd,khd->qhk", queries, keys, preferred_element_type=F32)
    scores = jnp.where(allowed[:, None, :], scores * head_width**-0.5, -1e30)
    top = jnp.max(scores, axis=2)
    weights = jnp.where(allowed[:, None, :], jnp.exp(scores - top[:, :, None]), 0.0)
    totals = jnp.sum(weights, axis=2)
    mixed_values = jnp.einsum(
        "qhk,khd->qhd", weights.astype(BF16), values, preferred_element_type=F32
    )
    attended = (mixed_values / totals[:, :, None]).astype(BF16).reshape(tok_count, -1)

    vmem = pl.BlockSpec(memory_space=pltpu.VMEM)
    dma = pltpu.SemaphoreType.DMA
    own_stream = lax.dynamic_slice_in_dim(stream, hid_index * rows, rows)
    x, sh = pl.pallas_call(
        functools.partial(mix_kernel, ns, hy, rows, slots, cols),
        out_shape=(
            jax.ShapeDtypeStruct((ns, slots, width), BF16),
            jax.ShapeDtypeStruct((HZ, tok_count, cols), F32),
        ),
        in_specs=[vmem] * 8,
        out_specs=(vmem, vmem),
        scratch_shapes=[
            pltpu.VMEM((HZ, hy - 1, rows, width), BF16),
            pltpu.VMEM((HZ, hy - 1, rows, width), BF16),
            pltpu.VMEM((HZ - 1, rows, width), BF16),
            pltpu.VMEM((HZ - 1, rows, width), BF16),
            pltpu.VMEM((tok_count, width), BF16),
            pltpu.VMEM((ns - 1, slots, width), BF16),
            pltpu.VMEM((ns - 1, slots, width), BF16),
            pltpu.VMEM((HZ, hy - 1, tok_count, cols), BF16),
            pltpu.VMEM((HZ, hy - 1, tok_count, cols), BF16),
            pltpu.VMEM((rows, width), F32),
            dma((HZ, hy - 1)), dma((HZ, hy - 1)),
            dma((HZ - 1,)), dma((HZ - 1,)),
            dma((HZ - 1,)), dma((HZ - 1,)),
            dma((HZ, hy - 1)), dma((HZ, hy - 1)),
            dma((ns - 1,)), dma((ns - 1,)),
            dma((HZ, hy - 1)), dma((HZ, hy - 1)),
        ],
        compiler_params=pltpu.CompilerParams(
            collective_id=0, has_side_effects=True, vmem_limit_bytes=48 * 2**20
        ),
    )(
        attended,
        out_proj.reshape(local_heads * head_width, width),
        own_stream,
        norm_gain.reshape(1, width),
        route,
        shared_gate,
        shared_up,
        shared_down,
    )

    x = x.reshape(ns, held, CAP, width)
    gate_local = gate_proj.reshape(held, units, width)
    up_local = up_proj.reshape(held, units, width)
    down_local = down_proj.reshape(held, units, width)
    gate_val = jnp.einsum("sicd,ifd->sicf", x, gate_local, preferred_element_type=F32)
    up_val = jnp.einsum("sicd,ifd->sicf", x, up_local, preferred_element_type=F32)
    act = (jax.nn.silu(gate_val) * up_val).astype(BF16)
    eo = jnp.einsum("sicf,ifd->sicd", act, down_local, preferred_element_type=F32)
    eo = eo.astype(BF16).reshape(ns, slots, width)

    count = ns * hy
    return pl.pallas_call(
        functools.partial(combine_kernel, ns, hy, slots, cols),
        out_shape=jax.ShapeDtypeStruct((tok_count, cols), BF16),
        in_specs=[vmem] * 3,
        out_specs=vmem,
        scratch_shapes=[
            pltpu.VMEM((HZ, count, slots, cols), BF16),
            pltpu.VMEM((HZ - 1, tok_count, cols), BF16),
            pltpu.VMEM((HZ - 1, tok_count, cols), BF16),
            dma((HZ, count)), dma((HZ, count)),
            dma((HZ - 1,)), dma((HZ - 1,)),
        ],
        compiler_params=pltpu.CompilerParams(
            collective_id=1, has_side_effects=True, vmem_limit_bytes=48 * 2**20
        ),
    )(eo, gates, sh)


def solution(mesh):
    placed = (
        P("seq", None),
        P("seq", "hid", None),
        P("seq", "hid", None),
        P("seq", "hid", None),
        P(),
        P("hid", None, None),
        P(),
        P("seq", None),
        P("seq", None),
        P(("seq", "hid"), None),
        P(("seq", "hid"), None),
        P(("seq", "hid"), None),
        P("hid", None),
        P("hid", None),
        P("hid", None),
    )
    return jax.shard_map(
        on_device, mesh=mesh, in_specs=placed, out_specs=P("seq", "hid"), check_vma=False
    )
```

time: 358 us -> 221 us (0.62); the launches traced: 353 us -> 221 us
  waiting for transfers between devices: 180 us -> 11.4 us
  Pallas kernels: 0 us -> 140 us
  local copies, waits for them, and re-layouts: 61.4 us -> 15.1 us
  other arithmetic: 36.4 us -> 12.3 us
  matrix products: 46.5 us -> 28.7 us
  starting transfers between devices: 15 us -> 0.01 us
    pallas_call x0 -> x2, Pallas kernels: none -> 140 us  [the longest x1 95.5 us: on_device(): pl.pallas_call(functools.partial(mix_kernel, ns, hy, rows, slots, cols),...]
    all_to_all x3 -> x0, waiting for transfers between devices: 91.3 us -> none  [the longest x1 55.1 us: on_device(): lax.all_to_all(down_part, 'hid', split_axis=0, concat_axis=0, tiled=True)]
    psum x1 -> x0, waiting for transfers between devices: 83.5 us -> none  [on_device(): lax.psum(partial_mix.astype(jnp.bfloat16), 'hid').astype(jnp.float32)]
    another operation x3 -> x0, other arithmetic: 18.5 us -> none
    dot_general x8 -> x9, matrix products: 46.5 us -> 28.7 us  [the longest x1 8.15 us: on_device(): jnp.einsum('sicd,ifd->sicf', x, up_local, preferred_element_type=F32)]
    gather x2 -> x0, local copies, waits for them, and re-layouts: 16.3 us -> none  [the longest x1 13 us: on_device(): picked = returned[pick_index].reshape(tok_count, TOP, col_count)]
    all_to_all x3 -> x0, starting transfers between devices: 14.9 us -> none  [the longest x1 5.3 us: on_device(): lax.all_to_all(send_rows, 'seq', split_axis=0, concat_axis=0, tiled=True)]
    scatter x1 -> x0, local copies, waits for them, and re-layouts: 12.1 us -> none  [on_device(): jnp.full((slot_total,), -1, jnp.int32).at[send_index]]
  transfers between devices with their start and end apart: 7 -> 1, of which waited for: 5 -> 1; matrix products, arithmetic and copies ran while one was open for 26% -> 6% of each run, Pallas kernels for 0% -> 0%
where the time goes in v1:
time: 221 us
  Pallas kernels  140 us (63%)
  matrix products  28.7 us (13%)
  local copies, waits for them, and re-layouts  15.1 us (7%)
  between operations  13.6 us (6%)
  other arithmetic  12.3 us (6%)
  waiting for transfers between devices  11.4 us (5%)
    pallas_call x1, Pallas kernels, on_device(): pl.pallas_call(functools.partial(mix_kernel, ns, hy, rows, slots, cols),...  95.5 us
    pallas_call x1, Pallas kernels, on_device(): pl.pallas_call(functools.partial(combine_kernel, ns, hy, slots, cols), ou...  44.4 us
    all_gather x1, waiting for transfers between devices, on_device(): both = lax.all_gather(both, 'seq', axis=0, tiled=True)  11.4 us
    dot_general x1, matrix products, on_device(): jnp.einsum('sicd,ifd->sicf', x, up_local, preferred_element_type=F32)  8.15 us
    dot_general x1, matrix products, on_device(): jnp.einsum('sicf,ifd->sicd', act, down_local, preferred_element_type=F32)  8.07 us
    dot_general x1, matrix products, on_device(): jnp.einsum('sicd,ifd->sicf', x, gate_local, preferred_element_type=F32)  7.72 us
    unnamed x31, local copies, waits for them, and re-layouts  5.62 us
    sub x1, other arithmetic, on_device(): scores - top[:, :, None]  4.91 us
  transfers between devices with their start and end apart: 1, of which 1 were waited for; matrix products, arithmetic and copies ran while one was open for 6% of the time, Pallas kernels for 0%

profile of v1, /device:TPU:9, one launch (start us, length us, event | category | flops | bytes accessed | tf_op | source)
XLA Modules:
  0.0 221.0 jit_solution(17048574420111857552)
XLA Ops:
  6.5 1.7 pad_maximum_fusion
  8.3 1.1 copy.37
  10.0 0.8 fusion.24
  11.3 1.6 eq.114
  12.8 2.9 %copy.45 = f32[512,1024]{1,0:T(8,128)} copy(f32[512,1024]{0,1:T(8,128)} %bitcast.69) | data formatting | bytes 4194304 | tf_op jit(solution)/shard_map/eq | solution.py:307
  16.1 1.3 copy.46
  17.8 1.0 fusion.23.route
  18.8 2.6 %select_convert_fusion.gates = bf16[512,1024]{1,0:T(8,128)(2,1)S(1)} fusion(bf16[512,1024]{1,0:T(8,128)(2,1)} %copy.46, f32[512,1024]{1,0:T(8,128)} %copy.45, f32[1024]{0:T(1024)S(1)} %eq.117), kind=kLoop, calls=%fused_computation.17 | loop fusion | flops 1048576 | bytes 4198400 | tf_op jit(solution)/shard_map/convert_element_type | solution.py:308
  21.4 1.0 fusion.6
  22.3 11.4 %all-gather.2.cloned.1.call-done = bf16[2048,512]{0,1:T(8,128)(2,1)} async-done(((bf16[512,512]{0,1:T(8,128)(2,1)}), bf16[2048,512]{0,1:T(8,128)(2,1)}) %all-gather.2.cloned.1.call-update) | async-done | bytes 2097168 | tf_op jit(solution)/shard_map/all_gather | solution.py:316
  33.7 2.5 %fusion.25 = f32[2,2048,512]{2,1,0:T(8,128)S(1)} fusion(bf16[2048,4,128]{0,2,1:T(8,128)(2,1)} %bitcast.72, bf16[512,2,128]{2,1,0:T(2,128)(2,1)S(1)} %copy-done.10), kind=kOutput, calls=%fused_computation.32 | convolution fusion | flops 536870912 | bytes 10747904 | tf_op jit(solution)/shard_map/qhd,khd->qhk/dot_general | solution.py:323
  36.3 4.9 %fusion.36 = (f32[512,2]{0,1:T(2,128)S(1)}, bf16[512,2,2048]{0,2,1:T(8,128)(2,1)S(1)}) fusion(f32[2,2048,512]{2,1,0:T(8,128)S(1)} %fusion.25, pred[512,2048]{0,1:T(8,128)(4,1)S(1)} %fusion.6), kind=kOutput, calls=%fused_computation.54 | output fusion | flops 16779264 | bytes 13635584 | tf_op jit(solution)/shard_map/sub | solution.py:326
  41.2 1.4 fusion.19
  42.7 1.8 copy.51.att
  44.5 1.4 copy-done.5
  45.8 1.2 copy-done.6
  47.0 0.9 copy-done.7
  48.0 95.5 %shard_map.145 = (bf16[4,128,2048]{2,1,0:T(8,128)(2,1)}, f32[4,512,256]{2,1,0:T(8,128)}) custom-call(bf16[512,256]{1,0:T(8,128)(2,1)S(1)} %copy-done.7, bf16[256,2048]{1,0:T(8,128)(2,1)S(1)} %bitcast.67, bf16[64,2048]{1,0:T(8,128)(2,1)S(1)} %constant_dynamic-slice_fusion.stream, f32[1,2048]{1,0:T(1,128)S(1)} %bitcast.68, bf16[512,512]{1,0:T(8,128)(2,1)S(1)} %copy-done.2, ...), custom_call_target="tpu_custom_call" | custom-call | tf_op jit(solution)/shard_map/pallas_call | solution.py:336
  143.5 7.7 %convolution_bitcast_fusion.1 = f32[4,2,64,1408]{3,2,0,1:T(8,128)S(1)} fusion(bf16[2,1408,2048,1]{2,1,3,0:T(8,128)(2,1)} %bitcast.75, bf16[4,2,64,2048]{3,2,1,0:T(8,128)(2,1)} %bitcast.78), kind=kOutput, calls=%fused_computation.13 | convolution fusion | flops 2952790016 | bytes 16515072 | tf_op jit(solution)/shard_map/sicd,ifd->sicf/dot_general | solution.py:380
  151.2 8.1 %fusion.9 = bf16[4,2,64,1408]{3,2,0,1:T(8,128)(2,1)S(1)} fusion(bf16[2,1408,2048,1]{2,1,3,0:T(8,128)(2,1)} %bitcast.76, f32[4,2,64,1408]{3,2,0,1:T(8,128)S(1)} %convolution_bitcast_fusion.1, bf16[4,2,64,2048]{3,2,1,0:T(8,128)(2,1)S(1)} %bitcast.79), kind=kOutput, calls=%fused_computation.14 | convolution fusion | flops 2957115392 | bytes 17956864 | tf_op jit(solution)/shard_map/sicd,ifd->sicf/dot_general | solution.py:381
  159.3 8.1 %fusion.10 = bf16[4,2,64,2048]{3,2,0,1:T(8,128)(2,1)S(1)} fusion(bf16[4,2,64,1408]{3,2,0,1:T(8,128)(2,1)S(1)} %fusion.9, bf16[2,1408,2048,1]{2,1,3,0:T(8,128)(2,1)} %bitcast.77), kind=kOutput, calls=%fused_computation.16 | convolution fusion | flops 2953838592 | bytes 15073280 | tf_op jit(solution)/shard_map/sicf,ifd->sicd/dot_general | solution.py:383
  167.7 1.3 copy-done.3
  169.0 44.4 %shard_map.146 = bf16[512,256]{1,0:T(8,128)(2,1)S(1)} custom-call(bf16[4,128,2048]{2,1,0:T(8,128)(2,1)S(1)} %bitcast.66, bf16[512,1024]{1,0:T(8,128)(2,1)S(1)} %select_convert_fusion.gates, f32[4,512,256]{2,1,0:T(8,128)S(1)} %copy-done.3), custom_call_target="tpu_custom_call" | custom-call | tf_op jit(solution)/shard_map/pallas_call | solution.py:387
  213.4 0.7 copy.60
  (51 shorter events, 2.0 us)
Async XLA Ops:
  6.5 12.2 %copy-start = (bf16[512,2048]{1,0:T(8,128)(2,1)S(1)}, bf16[512,2048]{1,0:T(8,128)(2,1)}, u32[]{:S(2)}) copy-start(bf16[512,2048]{1,0:T(8,128)(2,1)} %param.15) | copy-start | bytes 6291460
  6.5 27.2 %all-gather.2.cloned.1.call-start = ((), (), s32[]{:S(2)}) async-start(), calls=%async_computation | async-start | bytes 2621440 | tf_op jit(solution)/shard_map/all_gather | solution.py:316
  11.2 4.5 %copy-start.11 = (s32[512,6]{0,1:T(8,128)S(1)}, s32[512,6]{0,1:T(8,128)}, u32[]{:S(2)}) copy-start(s32[512,6]{0,1:T(8,128)} %param.22) | copy-start | bytes 36868
  11.2 4.5 %copy-start.12 = (f32[512,6]{0,1:T(8,128)S(1)}, f32[512,6]{0,1:T(8,128)}, u32[]{:S(2)}) copy-start(f32[512,6]{0,1:T(8,128)} %param.23) | copy-start | bytes 36868
  12.8 4.7 %copy-start.13 = (s32[2048]{0:T(1024)S(1)}, s32[2048]{0:T(1024)}, u32[]{:S(2)}) copy-start(s32[2048]{0:T(1024)} %param.19) | copy-start | bytes 24580
  18.8 14.9 %copy-start.10 = (bf16[512,2,128]{2,1,0:T(2,128)(2,1)S(1)}, bf16[512,2,128]{2,1,0:T(2,128)(2,1)}, u32[]{:S(2)}) copy-start(bf16[512,2,128]{2,1,0:T(2,128)(2,1)} %param.16) | copy-start | bytes 786436
  36.3 4.9 %copy-start.9 = (bf16[2048,512]{0,1:T(8,128)(2,1)S(1)}, bf16[2048,512]{0,1:T(8,128)(2,1)}, u32[]{:S(2)}) copy-start(bf16[2048,512]{0,1:T(8,128)(2,1)} %all-gather.2.cloned.1.call-done) | copy-start | bytes 6291460
  41.2 3.2 %copy-start.2 = (bf16[512,512]{1,0:T(8,128)(2,1)S(1)}, bf16[512,512]{1,0:T(8,128)(2,1)}, u32[]{:S(2)}) copy-start(bf16[512,512]{1,0:T(8,128)(2,1)} %fusion.23.route) | copy-start | bytes 1572868
  41.2 3.2 %copy-start.4 = (bf16[352,2048]{1,0:T(8,128)(2,1)S(1)}, bf16[352,2048]{1,0:T(8,128)(2,1)}, u32[]{:S(2)}) copy-start(bf16[352,2048]{1,0:T(8,128)(2,1)} %sg.1) | copy-start | bytes 4325380
  41.2 3.2 %copy-start.8 = (f32[2048]{0:T(1024)S(1)}, f32[2048]{0:T(1024)}, u32[]{:S(2)}) copy-start(f32[2048]{0:T(1024)} %param.21) | copy-start | bytes 24580
  44.4 1.4 copy-start.5
  45.8 1.2 copy-start.6
  47.0 0.9 copy-start.7
  143.5 7.7 %copy-start.14 = (bf16[4,128,2048]{2,1,0:T(8,128)(2,1)S(1)}, bf16[4,128,2048]{2,1,0:T(8,128)(2,1)}, u32[]{:S(2)}) copy-start(bf16[4,128,2048]{2,1,0:T(8,128)(2,1)} %get-tuple-element.7) | copy-start | bytes 6291460
  167.4 1.6 copy-start.3
  167.7 46.4 %copy-start.1 = (bf16[512,2048]{1,0:T(8,128)(2,1)S(1)}, bf16[512,2048]{1,0:T(8,128)(2,1)}, u32[]{:S(2)}) copy-start(bf16[512,2048]{1,0:T(8,128)(2,1)} %param.15) | copy-start | bytes 6291460
Sparse Core Ops, SparseCore 0:
  9.5 24.1 all-gather.1

commit v2 on v1

--- a/solution.py
+++ b/solution.py
@@ -40,14 +40,19 @@
 
 def mix_kernel(
     ns, hy, rows, slots, cols,
-    att, wout, stream, gain, route, sg, su, sd,
-    x_out, sh_out,
-    ysend, yrecv, zsend, zrecv, normed, dsend, drecv, ssend, srecv, mixed,
-    y_s, y_r, z_s, z_r, az_s, az_r, ay_s, ay_r, d_s, d_r, s_s, s_r,
+    att, wout, stream, gain, route, sg_hbm, su_hbm, sd_hbm,
+    x_out, sh_out, ss_out,
+    ysend, yrecv, zsend, zrecv, normed, dsend, drecv, mixed, sg, su, sd,
+    y_s, y_r, z_s, z_r, az_s, az_r, ay_s, ay_r, d_s, d_r, w_s,
 ):
     s = lax.axis_index("seq")
     h = lax.axis_index("hid")
     z, y = h // hy, lax.rem(h, hy)
+    loads = []
+    for i, (src, dst) in enumerate(((sg_hbm, sg), (su_hbm, su), (sd_hbm, sd))):
+        copy = pltpu.make_async_copy(src, dst, w_s.at[i])
+        copy.start()
+        loads.append(copy)
     for dz in range(1, HZ):
         greet(s, wrap(z + dz, HZ) * hy + y)
     for dy in range(1, hy):
@@ -132,6 +137,8 @@
     sent += to_seq
 
     nt = (((1,), (1,)), ((), ()))
+    for copy in loads:
+        copy.wait()
     gate_val = lax.dot_general(normed[...], sg[...], nt, preferred_element_type=F32)
     up_val = lax.dot_general(normed[...], su[...], nt, preferred_element_type=F32)
     act = (gate_val / (1.0 + jnp.exp(-gate_val)) * up_val).astype(BF16)
@@ -141,40 +148,45 @@
         hold[at_hold] = jnp.dot(act, sd[:, at_cols], preferred_element_type=F32)
         hold[at_hold, at(h), :] = hold[at_hold, at(h), :] + mixed[:, at_cols]
 
-    to_side = []
     for zt in range(HZ):
         for j in range(hy - 1):
-            yt = wrap(y + j + 1, hy)
-            shared(zt * hy + yt, sh_out, zt)
-            ssend[zt, j] = sh_out[zt].astype(BF16)
-            copy = remote(ssend.at[zt, j], srecv.at[zt, j], s_s.at[zt, j], s_r.at[zt, j], s, z * hy + yt)
-            copy.start()
-            to_side.append(copy)
-    sent += to_side
-    for zt in range(HZ):
+            shared(zt * hy + wrap(y + j + 1, hy), sh_out, zt)
+            ss_out[zt, j] = sh_out[zt].astype(BF16)
         shared(zt * hy + y, sh_out, zt)
-        for j in range(hy - 1):
-            to_side[zt * (hy - 1) + j].wait_recv()
-            sh_out[zt] = sh_out[zt] + srecv[zt, j].astype(F32)
-    x_out[s] = picked(s)
+
+    def keep(block, value):
+        for e in range(slots // CAP):
+            x_out[e, pl.ds(pl.multiple_of(block * CAP, CAP), CAP), :] = value[e * CAP : (e + 1) * CAP]
+
+    keep(s, picked(s))
     for k in range(ns - 1):
         to_seq[k].wait_recv()
-        x_out[wrap(s + k + 1, ns)] = drecv[k]
+        keep(wrap(s + k + 1, ns), drecv[k])
     for copy in sent:
         copy.wait_send()
 
 
-def combine_kernel(
-    ns, hy, slots, cols,
-    eo, gates, sh,
+def expert_kernel(
+    ns, hy, held, units, cols,
+    x, gates, sh, ss, gate_hbm, up_hbm, down_hbm,
     out,
-    recv, zsend, zrecv, l_s, l_r, z_s, z_r,
+    wg, wu, wd, act, eo, recv, zsend, zrecv, srecv,
+    w_s, l_s, l_r, z_s, z_r, s_s, s_r,
 ):
     s = lax.axis_index("seq")
     h = lax.axis_index("hid")
     z, y = h // hy, lax.rem(h, hy)
     layer = ns * hy
     me = s * hy + y
+    slots = held * CAP
+
+    loads = []
+    for e in range(held):
+        span = pl.ds(e * units, units)
+        for i, (src, dst) in enumerate(((gate_hbm, wg), (up_hbm, wu), (down_hbm, wd))):
+            copy = pltpu.make_async_copy(src.at[span], dst.at[span], w_s.at[e, i])
+            copy.start()
+            loads.append(copy)
 
     def hello(k, carry):
         peer = lax.rem(me + k, layer)
@@ -186,36 +198,80 @@
         greet(s, wrap(z + dz, HZ) * hy + y)
     pl.semaphore_wait(pltpu.get_barrier_semaphore(), layer - 1 + HZ - 1)
 
-    def chunk(block, hid):
-        return eo.at[block, :, pl.ds(pl.multiple_of(hid * cols, cols), cols)]
-
-    def outgoing(i, k):
-        zt = wrap(z + i + 1, HZ)
-        peer = lax.rem(me + k, layer)
-        block, yt = peer // hy, lax.rem(peer, hy)
-        return remote(chunk(block, zt * hy + yt), recv.at[i, me], l_s.at[i, k], l_r.at[i, k], block, z * hy + yt)
-
-    def incoming(i, k):
-        peer = lax.rem(me + layer - k, layer)
-        return remote(recv.at[i, peer], recv.at[i, peer], l_s.at[i, k], l_r.at[i, k], s, h)
-
-    for i in range(HZ):
-        def start(k, carry, i=i):
-            outgoing(i, layer - k).start()
+    to_side = []
+    for i in range(HZ):
+        zt = wrap(z + i + 1, HZ)
+        for j in range(hy - 1):
+            copy = remote(
+                ss.at[zt, j], srecv.at[i, j], s_s.at[i, j], s_r.at[i, j],
+                s, z * hy + wrap(y + j + 1, hy),
+            )
+            copy.start()
+            to_side.append(copy)
+
+    nt = (((1,), (1,)), ((), ()))
+    for e in range(held):
+        loads[3 * e].wait()
+        loads[3 * e + 1].wait()
+
+        def hidden(first, size, e=e):
+            span = pl.ds(e * units + first, size)
+            gate_val = lax.dot_general(x[e], wg[span, :], nt, preferred_element_type=F32)
+            up_val = lax.dot_general(x[e], wu[span, :], nt, preferred_element_type=F32)
+            value = gate_val / (1.0 + jnp.exp(-gate_val)) * up_val
+            act[e, :, pl.ds(first, size)] = value.astype(BF16)
+
+        def tile(n, carry, hidden=hidden):
+            hidden(pl.multiple_of(n * 256, 128), 256)
             return carry
 
-        lax.fori_loop(1, layer, start, 0)
-        recv[i, me] = eo[s, :, pl.ds(pl.multiple_of((wrap(z + i + 1, HZ) * hy + y) * cols, cols), cols)]
+        lax.fori_loop(0, units // 256, tile, 0)
+        if units % 256:
+            hidden(units // 256 * 256, units % 256)
+    for e in range(held):
+        loads[3 * e + 2].wait()
+
+    def outgoing(i, j, k):
+        block, yt = lax.rem(s + k, ns), wrap(y + j, hy)
+        return remote(
+            eo.at[i, j, block], recv.at[i, me], l_s.at[i, j, k], l_r.at[i, j, k],
+            block, z * hy + yt,
+        )
+
+    def incoming(i, j, k):
+        peer = lax.rem(s + ns - k, ns) * hy + wrap(y - j, hy)
+        return remote(recv.at[i, peer], recv.at[i, peer], l_s.at[i, j, k], l_r.at[i, j, k], s, h)
+
+    def every(action, i, j):
+        def one(k, carry):
+            action(i, j, k)
+            return carry
+
+        lax.fori_loop(1 if j == 0 else 0, ns, one, 0)
+
+    for i in range(HZ):
+        zt = wrap(z + i + 1, HZ)
+        for j in reversed(range(hy)):
+            hid = zt * hy + wrap(y + j, hy)
+            span = pl.ds(pl.multiple_of(hid * cols, cols), cols)
+            for e in range(held):
+                value = jnp.dot(
+                    act[e], wd[pl.ds(e * units, units), span], preferred_element_type=F32
+                )
+                eo[i, j, :, e * CAP : (e + 1) * CAP, :] = value.astype(BF16).reshape(ns, CAP, cols)
+            every(lambda i, j, k: outgoing(i, j, k).start(), i, j)
+        recv[i, me] = eo[i, 0, s]
 
     to_z, total = [], None
     for i in range(HZ):
-        def land(k, carry, i=i):
-            incoming(i, layer - k).wait_recv()
-            return carry
-
-        lax.fori_loop(1, layer, land, 0)
-        zt = wrap(z + i + 1, HZ)
-        total = sh[zt] + jnp.dot(
+        zt = wrap(z + i + 1, HZ)
+        total = sh[zt]
+        for j in range(hy - 1):
+            to_side[i * (hy - 1) + j].wait_recv()
+            total = total + srecv[i, j].astype(F32)
+        for j in range(hy):
+            every(lambda i, j, k: incoming(i, j, k).wait_recv(), i, j)
+        total = total + jnp.dot(
             gates[...], recv[i].reshape(layer * slots, cols), preferred_element_type=F32
         )
         if i < HZ - 1:
@@ -228,12 +284,9 @@
         total = total + zrecv[i].astype(F32)
     out[...] = total.astype(BF16)
     for i in range(HZ):
-        def left(k, carry, i=i):
-            outgoing(i, k).wait_send()
-            return carry
-
-        lax.fori_loop(1, layer, left, 0)
-    for copy in to_z:
+        for j in range(hy):
+            every(lambda i, j, k: outgoing(i, j, k).wait_send(), i, j)
+    for copy in to_z + to_side:
         copy.wait_send()
 
 
@@ -331,16 +384,18 @@
     attended = (mixed_values / totals[:, :, None]).astype(BF16).reshape(tok_count, -1)
 
     vmem = pl.BlockSpec(memory_space=pltpu.VMEM)
+    hbm = pl.BlockSpec(memory_space=pl.ANY)
     dma = pltpu.SemaphoreType.DMA
     own_stream = lax.dynamic_slice_in_dim(stream, hid_index * rows, rows)
-    x, sh = pl.pallas_call(
+    x, sh, ss = pl.pallas_call(
         functools.partial(mix_kernel, ns, hy, rows, slots, cols),
         out_shape=(
-            jax.ShapeDtypeStruct((ns, slots, width), BF16),
+            jax.ShapeDtypeStruct((held, ns * CAP, width), BF16),
             jax.ShapeDtypeStruct((HZ, tok_count, cols), F32),
+            jax.ShapeDtypeStruct((HZ, hy - 1, tok_count, cols), BF16),
         ),
-        in_specs=[vmem] * 8,
-        out_specs=(vmem, vmem),
+        in_specs=[vmem] * 5 + [hbm] * 3,
+        out_specs=(vmem, vmem, vmem),
         scratch_shapes=[
             pltpu.VMEM((HZ, hy - 1, rows, width), BF16),
             pltpu.VMEM((HZ, hy - 1, rows, width), BF16),
@@ -349,15 +404,15 @@
             pltpu.VMEM((tok_count, width), BF16),
             pltpu.VMEM((ns - 1, slots, width), BF16),
             pltpu.VMEM((ns - 1, slots, width), BF16),
-            pltpu.VMEM((HZ, hy - 1, tok_count, cols), BF16),
-            pltpu.VMEM((HZ, hy - 1, tok_count, cols), BF16),
             pltpu.VMEM((rows, width), F32),
+            pltpu.VMEM(shared_gate.shape, BF16),
+            pltpu.VMEM(shared_up.shape, BF16),
+            pltpu.VMEM(shared_down.shape, BF16),
             dma((HZ, hy - 1)), dma((HZ, hy - 1)),
             dma((HZ - 1,)), dma((HZ - 1,)),
             dma((HZ - 1,)), dma((HZ - 1,)),
             dma((HZ, hy - 1)), dma((HZ, hy - 1)),
-            dma((ns - 1,)), dma((ns - 1,)),
-            dma((HZ, hy - 1)), dma((HZ, hy - 1)),
+            dma((ns - 1,)), dma((ns - 1,)), dma((3,)),
         ],
         compiler_params=pltpu.CompilerParams(
             collective_id=0, has_side_effects=True, vmem_limit_bytes=48 * 2**20
@@ -373,33 +428,31 @@
         shared_down,
     )
 
-    x = x.reshape(ns, held, CAP, width)
-    gate_local = gate_proj.reshape(held, units, width)
-    up_local = up_proj.reshape(held, units, width)
-    down_local = down_proj.reshape(held, units, width)
-    gate_val = jnp.einsum("sicd,ifd->sicf", x, gate_local, preferred_element_type=F32)
-    up_val = jnp.einsum("sicd,ifd->sicf", x, up_local, preferred_element_type=F32)
-    act = (jax.nn.silu(gate_val) * up_val).astype(BF16)
-    eo = jnp.einsum("sicf,ifd->sicd", act, down_local, preferred_element_type=F32)
-    eo = eo.astype(BF16).reshape(ns, slots, width)
-
     count = ns * hy
     return pl.pallas_call(
-        functools.partial(combine_kernel, ns, hy, slots, cols),
+        functools.partial(expert_kernel, ns, hy, held, units, cols),
         out_shape=jax.ShapeDtypeStruct((tok_count, cols), BF16),
-        in_specs=[vmem] * 3,
+        in_specs=[vmem] * 4 + [hbm] * 3,
         out_specs=vmem,
         scratch_shapes=[
+            pltpu.VMEM((unit_rows, width), BF16),
+            pltpu.VMEM((unit_rows, width), BF16),
+            pltpu.VMEM((unit_rows, width), BF16),
+            pltpu.VMEM((held, ns * CAP, units), BF16),
+            pltpu.VMEM((HZ, hy, ns, slots, cols), BF16),
             pltpu.VMEM((HZ, count, slots, cols), BF16),
             pltpu.VMEM((HZ - 1, tok_count, cols), BF16),
             pltpu.VMEM((HZ - 1, tok_count, cols), BF16),
-            dma((HZ, count)), dma((HZ, count)),
+            pltpu.VMEM((HZ, hy - 1, tok_count, cols), BF16),
+            dma((held, 3)),
+            dma((HZ, hy, ns)), dma((HZ, hy, ns)),
             dma((HZ - 1,)), dma((HZ - 1,)),
+            dma((HZ, hy - 1)), dma((HZ, hy - 1)),
         ],
         compiler_params=pltpu.CompilerParams(
-            collective_id=1, has_side_effects=True, vmem_limit_bytes=48 * 2**20
+            collective_id=1, has_side_effects=True, vmem_limit_bytes=58 * 2**20
         ),
-    )(eo, gates, sh)
+    )(x, gates, sh, ss, gate_proj, up_proj, down_proj)
 
 
 def solution(mesh):

time: 221 us -> 224 us (1.014)
  Pallas kernels: 140 us -> 169 us
  matrix products: 28.7 us -> 4.04 us
    pallas_call x1, Pallas kernels: 44.4 us -> 79.2 us  [on_device(): pl.pallas_call(functools.partial(expert_kernel, ns, hy, held, units, cols...]
    dot_general x3 -> x0, matrix products: 23.9 us -> none  [the longest x1 8.15 us: on_device(): jnp.einsum('sicd,ifd->sicf', x, up_local, preferred_element_type=F32)]
    pallas_call x1, Pallas kernels: 95.5 us -> 90.1 us  [on_device(): pl.pallas_call(functools.partial(mix_kernel, ns, hy, rows, slots, cols),...]
    unnamed x31 -> x23, local copies, waits for them, and re-layouts: 5.62 us -> 5.75 us
where the time goes in v2:
time: 224 us
  Pallas kernels  169 us (75%)
  between operations  13.6 us (6%)
  local copies, waits for them, and re-layouts  13.3 us (6%)
  other arithmetic  12.4 us (6%)
  waiting for transfers between devices  11.1 us (5%)
  matrix products  4.04 us (2%)
    pallas_call x1, Pallas kernels, on_device(): pl.pallas_call(functools.partial(mix_kernel, ns, hy, rows, slots, cols),...  90.1 us
    pallas_call x1, Pallas kernels, on_device(): pl.pallas_call(functools.partial(expert_kernel, ns, hy, held, units, cols...  79.2 us
    all_gather x1, waiting for transfers between devices, on_device(): both = lax.all_gather(both, 'seq', axis=0, tiled=True)  11.1 us
    unnamed x23, local copies, waits for them, and re-layouts  5.75 us
    sub x1, other arithmetic, on_device(): scores - top[:, :, None]  4.73 us
    eq x4, local copies, waits for them, and re-layouts, on_device(): rank_layer[:, :, None] == slot[None, None, :]  4.56 us
  transfers between devices with their start and end apart: 1, of which 1 were waited for; matrix products, arithmetic and copies ran while one was open for 6% of the time, Pallas kernels for 0%

profile of v2, /device:TPU:9, one launch (start us, length us, event | category | flops | bytes accessed | tf_op | source)
XLA Modules:
  0.0 223.8 jit_solution(17047490901322261718)
XLA Ops:
  6.5 1.7 pad_maximum_fusion
  8.3 1.1 copy.33
  9.9 0.8 select_reduce_fusion
  10.8 0.2 fusion.22
  11.1 1.3 copy.39
  12.5 0.3 fusion.17
  12.8 0.2 fusion.24
  13.0 1.6 eq.114
  14.6 2.9 %copy.38 = f32[512,1024]{1,0:T(8,128)} copy(f32[512,1024]{0,1:T(8,128)} %bitcast.37) | data formatting | bytes 4194304 | tf_op jit(solution)/shard_map/eq | solution.py:360
  17.6 0.2 fusion.25
  17.8 0.2 fusion.18.route
  18.0 3.6 %select_convert_fusion.gates = bf16[512,1024]{1,0:T(8,128)(2,1)} fusion(bf16[512,1024]{1,0:T(8,128)(2,1)} %copy.39, f32[512,1024]{1,0:T(8,128)} %copy.38, f32[1024]{0:T(1024)S(1)} %eq.117), kind=kLoop, calls=%fused_computation.11 | loop fusion | flops 1048576 | bytes 4198400 | tf_op jit(solution)/shard_map/convert_element_type | solution.py:361
  21.7 0.9 fusion.6
  22.6 11.1 %all-gather.2.cloned.1.call-done = bf16[2048,512]{0,1:T(8,128)(2,1)} async-done(((bf16[512,512]{0,1:T(8,128)(2,1)}), bf16[2048,512]{0,1:T(8,128)(2,1)}) %all-gather.2.cloned.1.call-update) | async-done | bytes 2097168 | tf_op jit(solution)/shard_map/all_gather | solution.py:369
  33.7 2.5 %fusion.20 = f32[2,2048,512]{2,1,0:T(8,128)S(1)} fusion(bf16[2048,4,128]{0,2,1:T(8,128)(2,1)} %bitcast.40, bf16[512,2,128]{2,1,0:T(2,128)(2,1)S(1)} %copy-done.8), kind=kOutput, calls=%fused_computation.24 | convolution fusion | flops 536870912 | bytes 10747904 | tf_op jit(solution)/shard_map/qhd,khd->qhk/dot_general | solution.py:376
  36.2 4.7 %fusion.31 = (f32[512,2]{0,1:T(2,128)S(1)}, bf16[512,2,2048]{0,2,1:T(8,128)(2,1)S(1)}) fusion(f32[2,2048,512]{2,1,0:T(8,128)S(1)} %fusion.20, pred[512,2048]{0,1:T(8,128)(4,1)S(1)} %fusion.6), kind=kOutput, calls=%fused_computation.46 | output fusion | flops 16779264 | bytes 13635584 | tf_op jit(solution)/shard_map/sub | solution.py:379
  41.0 0.7 fusion.14
  41.9 0.5 copy-done.2
  42.4 1.4 copy-done.3
  43.7 1.2 copy-done.4
  44.9 90.1 %shard_map.145 = (bf16[2,256,2048]{2,1,0:T(8,128)(2,1)}, f32[4,512,256]{2,1,0:T(8,128)}, bf16[4,1,512,256]{3,2,1,0:T(8,128)(2,1)S(1)}) custom-call(bf16[512,256]{1,0:T(8,128)(2,1)S(1)} %copy.41.att, bf16[256,2048]{1,0:T(8,128)(2,1)S(1)} %bitcast.35, bf16[64,2048]{1,0:T(8,128)(2,1)S(1)} %constant_dynamic-slice_fusion.stream, f32[1,2048]{1,0:T(1,128)S(1)} %bitcast.36, ...), custom_call_target="tpu_custom_call" | custom-call | tf_op jit(solution)/shard_map/pallas_call | solution.py:390
  135.1 1.0 copy-done.5
  136.1 79.2 %shard_map.146 = bf16[512,256]{1,0:T(8,128)(2,1)} custom-call(bf16[2,256,2048]{2,1,0:T(8,128)(2,1)} %get-tuple-element.8.x, bf16[512,1024]{1,0:T(8,128)(2,1)} %select_convert_fusion.gates, f32[4,512,256]{2,1,0:T(8,128)} %get-tuple-element.9.sh, bf16[4,1,512,256]{3,2,1,0:T(8,128)(2,1)} %copy-done.5, bf16[2816,2048]{1,0:T(8,128)(2,1)} %gate_hbm.1, ...), custom_call_target="tpu_custom_call" | custom-call | tf_op jit(solution)/shard_map/pallas_call | solution.py:432
  215.3 1.7 copy.46
  (39 shorter events, 1.1 us)
Async XLA Ops:
  6.5 11.4 %copy-start = (bf16[512,2048]{1,0:T(8,128)(2,1)S(1)}, bf16[512,2048]{1,0:T(8,128)(2,1)}, u32[]{:S(2)}) copy-start(bf16[512,2048]{1,0:T(8,128)(2,1)} %param.15) | copy-start | bytes 6291460
  6.5 5.9 %copy-start.9 = (s32[512,6]{0,1:T(8,128)S(1)}, s32[512,6]{0,1:T(8,128)}, u32[]{:S(2)}) copy-start(s32[512,6]{0,1:T(8,128)} %param.22) | copy-start | bytes 36868
  6.5 27.2 %all-gather.2.cloned.1.call-start = ((), (), s32[]{:S(2)}) async-start(), calls=%async_computation | async-start | bytes 2621440 | tf_op jit(solution)/shard_map/all_gather | solution.py:369
  11.1 6.5 %copy-start.10 = (s32[2048]{0:T(1024)S(1)}, s32[2048]{0:T(1024)}, u32[]{:S(2)}) copy-start(s32[2048]{0:T(1024)} %param.19) | copy-start | bytes 24580
  17.5 16.3 %copy-start.8 = (bf16[512,2,128]{2,1,0:T(2,128)(2,1)S(1)}, bf16[512,2,128]{2,1,0:T(2,128)(2,1)}, u32[]{:S(2)}) copy-start(bf16[512,2,128]{2,1,0:T(2,128)(2,1)} %param.16) | copy-start | bytes 786436
  36.2 4.7 %copy-start.7 = (bf16[2048,512]{0,1:T(8,128)(2,1)S(1)}, bf16[2048,512]{0,1:T(8,128)(2,1)}, u32[]{:S(2)}) copy-start(bf16[2048,512]{0,1:T(8,128)(2,1)} %all-gather.2.cloned.1.call-done) | copy-start | bytes 6291460
  41.0 1.4 copy-start.2
  41.0 1.4 copy-start.6
  42.3 1.4 copy-start.3
  43.7 1.2 copy-start.4
  135.1 1.0 copy-start.5
  136.1 80.9 %copy-start.1 = (bf16[512,2048]{1,0:T(8,128)(2,1)S(1)}, bf16[512,2048]{1,0:T(8,128)(2,1)}, u32[]{:S(2)}) copy-start(bf16[512,2048]{1,0:T(8,128)(2,1)} %param.15) | copy-start | bytes 6291460
Sparse Core Ops, SparseCore 0:
  9.5 24.1 all-gather.1
